TPU v7x, 512 devices: a whole 4x8x8 slice. The times are simulated.
512 devices in a mesh: slab: 128 (over y, z, core), grp: 4 (over x).
Axes of the slice: x: 4, y: 8, z: 8, core: 2. Of those that a mesh axis runs over, the one named last changes fastest.
Arguments:
- u_now: float32 [3, 2048, 32, 128], P(None, 'slab', 'grp'), may hold values from -6 to 6
- u_prev: float32 [3, 2048, 32, 128], P(None, 'slab', 'grp'), may hold values from -6 to 6
- force: float32 [3, 2048, 32, 128], P(None, 'slab', 'grp'), may hold values from -6 to 6
- stiffness: float32 [2048, 32, 128], P('slab', 'grp'), may hold values from 0.5 to 2
- broken: int32 [512, 8, 32], P('slab', 'grp'), may hold values 0 or 1
- flags: int32 [512, 8, 32], P('slab', 'grp'), may hold values 0 or 1
Outputs:
- displacement: float32 [3, 2048, 32, 128], P(None, 'slab', 'grp')
- coeffs: float32 [6, 32, 128, 2048], P(None, 'grp', 'slab')
All inputs are finite; a program needn't handle non-finite values. No bound on the sum of `broken` or of `flags` on one device may be relied on, other than what follows from the above.
Results may differ from a plain program's by a relative error of at most 0.0001.
Values sent between devices are 32-bit elements; how exact they have to be, the bound alone decides.
No kernel may reach another device: no remote copies, remote signals or barrier semaphores. Data moves between devices by JAX's collectives and lax.ppermute only.
A program may use at most 64 MiB of HBM per device.

v0:
```python
import jax
import jax.numpy as jnp
import numpy as np
from jax import lax
from jax.sharding import PartitionSpec as P

STEPS = 2
ITERS = 2
LEVELS = 3
SPRING_NORMAL = 1.0
SPRING_SHEAR = 0.4
MASS_TERM = 1.0
CRACK_CUT = 0.9


def with_halo(block, sides, width):
    for axis, dim in sides:
        count = lax.axis_size(axis)
        forward = [(i, i + 1) for i in range(count - 1)]
        backward = [(target, source) for source, target in forward]
        low = lax.ppermute(
            lax.slice_in_dim(block, block.shape[dim] - width, None, axis=dim), axis, forward
        )
        high = lax.ppermute(lax.slice_in_dim(block, 0, width, axis=dim), axis, backward)
        block = jnp.concatenate([low, block, high], axis=dim)
    return block


def cosine_table():
    freq = np.arange(4)[:, None]
    place = np.arange(4)[None, :]
    factor = np.where(freq == 0, 0.5, np.sqrt(0.5))
    return factor * np.cos(np.pi * (2 * place + 1) * freq / 8.0)


def block_table(count):
    return jnp.asarray(np.kron(np.eye(count // 4), cosine_table()), jnp.float32)


def spread(mask):
    values = mask.astype(jnp.float32)
    size_a, size_b, size_c = values.shape
    wide = jnp.broadcast_to(values[:, None, :, None, :, None], (size_a, 4, size_b, 4, size_c, 4))
    return wide.reshape(size_a * 4, size_b * 4, size_c * 4)


def sides(padded, axis_index):
    leading = padded.ndim - 3

    def cut(offset):
        index_list = [slice(None)] * leading + [slice(1, -1)] * 3
        length = padded.shape[leading + axis_index]
        index_list[leading + axis_index] = slice(1 + offset, length - 1 + offset)
        return padded[tuple(index_list)]

    return (cut(1), cut(-1))


def springs(field, weight, field_pad, weight_pad):
    result = MASS_TERM * field
    for axis_index in range(3):
        upper_v, lower_v = sides(field_pad, axis_index)
        upper_w, lower_w = sides(weight_pad, axis_index)
        k_upper = 0.5 * (weight + upper_w)
        k_lower = 0.5 * (weight + lower_w)
        change = k_upper * (field - upper_v) + k_lower * (field - lower_v)
        coupling = jnp.array(
            [SPRING_NORMAL if comp == axis_index else SPRING_SHEAR for comp in range(3)],
            jnp.float32,
        ).reshape(3, 1, 1, 1)
        result = result + coupling * change
    return result


def faces(field):
    padded = with_halo(field, (("slab", 1), ("grp", 2)), 1)
    return jnp.pad(padded, ((0, 0), (0, 0), (0, 0), (1, 1)))


def stresses(carry, field_pad):
    rows_out = []
    for axis_index in range(3):
        upper_v, lower_v = sides(field_pad, axis_index)
        rows_out.append(SPRING_NORMAL * carry * 0.5 * (upper_v[axis_index] - lower_v[axis_index]))
    return jnp.stack(rows_out)


def single_sum(value):
    return lax.psum(value, ("slab", "grp"))


def lift(signal):
    even = signal[..., 0::2]
    odd = signal[..., 1::2]
    detail = odd - 0.5 * (even + jnp.roll(even, -1, axis=-1))
    approx = even + 0.25 * (jnp.roll(detail, 1, axis=-1) + detail)
    return (approx, detail)


def wavelet(signal):
    pieces = []
    approx = signal
    for level_index in range(LEVELS):
        approx, detail = lift(approx)
        pieces.insert(0, detail)
    return jnp.concatenate([approx] + pieces, axis=-1)


def body(u_now, u_prev, force, stiffness, broken, flags):
    weight = stiffness * (1.0 - CRACK_CUT * spread(broken))
    carry = spread(flags) * weight
    weight_pad = with_halo(weight, (("slab", 0), ("grp", 1)), 1)
    weight_pad = jnp.pad(weight_pad, ((0, 0), (0, 0), (1, 1)))

    def operate(field):
        return springs(field, weight, faces(field), weight_pad)

    for step_index in range(STEPS):
        rhs = MASS_TERM * (2.0 * u_now - u_prev) + force
        guess = u_now
        residual = rhs - operate(guess)
        direction = residual
        norm_now = single_sum(jnp.sum(residual * residual))
        for turn_index in range(ITERS):
            image = operate(direction)
            alpha = norm_now / single_sum(jnp.sum(direction * image))
            guess = guess + alpha * direction
            residual = residual - alpha * image
            if turn_index + 1 < ITERS:
                norm_next = single_sum(jnp.sum(residual * residual))
                direction = residual + norm_next / norm_now * direction
                norm_now = norm_next
        u_prev = u_now
        u_now = guess
    stress = stresses(carry, faces(u_now))
    fields = jnp.concatenate([u_now, stress], axis=0)
    table_x = block_table(fields.shape[1])
    table_y = block_table(fields.shape[2])
    table_z = block_table(fields.shape[3])
    blockc = jnp.einsum("ax,hxyz->hayz", table_x, fields, precision=lax.Precision.HIGHEST)
    blockc = jnp.einsum("by,hxyz->hxbz", table_y, blockc, precision=lax.Precision.HIGHEST)
    blockc = jnp.einsum("hxyz,cz->hxyc", blockc, table_z, precision=lax.Precision.HIGHEST)
    moved = jnp.transpose(blockc, (0, 2, 3, 1))
    shipped = lax.all_to_all(moved, "slab", split_axis=2, concat_axis=3, tiled=True)
    coeffs = wavelet(shipped)
    return (u_now, coeffs)


def solution(mesh):
    return jax.shard_map(
        body,
        mesh=mesh,
        in_specs=(
            P(None, "slab", "grp", None),
            P(None, "slab", "grp", None),
            P(None, "slab", "grp", None),
            P("slab", "grp", None),
            P("slab", "grp", None),
            P("slab", "grp", None),
        ),
        out_specs=(P(None, "slab", "grp", None), P(None, "grp", "slab", None)),
        check_vma=False,
    )
```

profile of v0, /device:TPU:1, one launch (start us, length us, event | category | flops | bytes accessed | tf_op | source)
XLA Modules:
  0.0 816.2 jit_solution(5298064619461524530)
XLA Ops:
  3.5 5.4 collective-permute-start.2
  8.9 4.7 collective-permute-start
  13.6 1.9 collective-permute-start.1
  15.5 3.6 collective-permute-start.3
  21.9 4.0 collective-permute-start.7
  27.5 3.4 collective-permute-done.5
  31.6 3.8 collective-permute-start.9
  35.4 1.9 collective-permute-start.8
  37.3 3.1 collective-permute-done.8
  40.4 3.1 collective-permute-start.11
  44.8 3.4 collective-permute-done.10
  49.5 106.3 %all-reduce.9 = (f32[]{:T(128)}, f32[]{:T(128)}) all-reduce(f32[]{:T(128)} %get-tuple-element.11, f32[]{:T(128)} %get-tuple-element.10), channel_id=1, replica_groups=mesh['slab'=128,'grp'=4] {'slab','grp'}, use_global_device_ids=true, to_apply=%region_1.2 | all-reduce | flops 2 | bytes 16 | tf_op jit(solution)/shard_map/psum | solution.py:89
  157.7 95.6 %psum.58 = f32[]{:T(128)} all-reduce(f32[]{:T(128)} %multiply_reduce_fusion.3), channel_id=1, replica_groups=mesh['slab'=128,'grp'=4] {'slab','grp'}, use_global_device_ids=true, to_apply=%region_5.6 | all-reduce | flops 1 | bytes 8 | tf_op jit(solution)/shard_map/psum | solution.py:89
  254.8 2.2 collective-permute-start.13
  257.0 2.1 collective-permute-start.12
  259.1 2.9 collective-permute-done.12
  262.0 2.8 collective-permute-start.15
  266.1 3.4 collective-permute-done.14
  270.7 100.4 %psum.59 = f32[]{:T(128)} all-reduce(f32[]{:T(128)} %fusion.75), channel_id=1, replica_groups=mesh['slab'=128,'grp'=4] {'slab','grp'}, use_global_device_ids=true, to_apply=%region_7.8 | all-reduce | flops 1 | bytes 8 | tf_op jit(solution)/shard_map/psum | solution.py:89
  372.6 1.9 collective-permute-start.17
  374.5 2.4 collective-permute-start.16
  376.9 2.6 collective-permute-done.16
  379.6 3.7 collective-permute-start.19
  384.6 3.4 collective-permute-done.18
  388.6 3.6 collective-permute-start.21
  392.2 1.9 collective-permute-start.20
  394.2 3.1 collective-permute-done.20
  400.0 3.4 collective-permute-done.22
  404.7 105.3 %all-reduce.8 = (f32[]{:T(128)}, f32[]{:T(128)}) all-reduce(f32[]{:T(128)} %get-tuple-element.9, f32[]{:T(128)} %get-tuple-element.8), channel_id=1, replica_groups=mesh['slab'=128,'grp'=4] {'slab','grp'}, use_global_device_ids=true, to_apply=%region_9.10 | all-reduce | flops 2 | bytes 16 | tf_op jit(solution)/shard_map/psum | solution.py:89
  511.9 95.4 %psum.62 = f32[]{:T(128)} all-reduce(f32[]{:T(128)} %multiply_reduce_fusion), channel_id=1, replica_groups=mesh['slab'=128,'grp'=4] {'slab','grp'}, use_global_device_ids=true, to_apply=%region_13.14 | all-reduce | flops 1 | bytes 8 | tf_op jit(solution)/shard_map/psum | solution.py:89
  608.7 2.2 collective-permute-start.25
  611.0 2.1 collective-permute-start.24
  613.1 2.9 collective-permute-done.24
  616.0 3.4 collective-permute-start.27
  620.7 3.4 collective-permute-done.26
  625.4 100.4 %psum.63 = f32[]{:T(128)} all-reduce(f32[]{:T(128)} %fusion.15), channel_id=1, replica_groups=mesh['slab'=128,'grp'=4] {'slab','grp'}, use_global_device_ids=true, to_apply=%region_15.16 | all-reduce | flops 1 | bytes 8 | tf_op jit(solution)/shard_map/psum | solution.py:89
  729.2 2.4 collective-permute-start.28
  731.6 2.6 collective-permute-done.28
  734.2 3.7 collective-permute-start.31
  745.3 2.1 copy.79
  749.3 14.6 %all-to-all-start = ((f32[128,1,768]{2,1,0:T(1,128)}), f32[128,1,768]{2,1,0:T(1,128)S(1)}, u32[]{:S(2)}, u32[]{:S(2)}) async-start(f32[128,1,768]{2,1,0:T(1,128)} %reshape.66), calls=%async_computation | async-start | bytes 786432 | tf_op jit(solution)/shard_map/all_to_all | solution.py:144
  764.7 16.0 %all-to-all-done = f32[128,1,768]{2,1,0:T(1,128)S(1)} async-done(((f32[128,1,768]{2,1,0:T(1,128)}), f32[128,1,768]{2,1,0:T(1,128)S(1)}, u32[]{:S(2)}, u32[]{:S(2)}) %all-to-all-start) | async-done | bytes 393248 | tf_op jit(solution)/shard_map/all_to_all | solution.py:144
  783.8 2.6 copy.80
  786.4 3.8 all_to_all.10
  790.1 6.7 slice.508
  796.8 6.9 slice.509
  804.1 3.3 slice.514
  807.4 3.3 slice.515
  (126 shorter events, 43.5 us)
Async XLA Ops:
  0.6 2.8 copy-start.3
  0.6 12.9 %copy-start = (f32[3,16,8,128]{3,2,1,0:T(8,128)S(1)}, f32[3,16,8,128]{3,2,1,0:T(8,128)}, u32[]{:S(2)}) copy-start(f32[3,16,8,128]{3,2,1,0:T(8,128)} %param.27) | copy-start | bytes 589828
  1.7 29.5 %copy-start.1 = (f32[3,16,8,128]{3,2,1,0:T(8,128)S(1)}, f32[3,16,8,128]{3,2,1,0:T(8,128)}, u32[]{:S(2)}) copy-start(f32[3,16,8,128]{3,2,1,0:T(8,128)} %param.29) | copy-start | bytes 589828
  1.7 29.5 %copy-start.2 = (f32[3,16,8,128]{3,2,1,0:T(8,128)S(1)}, f32[3,16,8,128]{3,2,1,0:T(8,128)}, u32[]{:S(2)}) copy-start(f32[3,16,8,128]{3,2,1,0:T(8,128)} %param.28) | copy-start | bytes 589828
  1.7 29.5 %copy-start.5 = (f32[3]{0:T(128)S(1)}, f32[3]{0:T(128)}, u32[]{:S(2)}) copy-start(f32[3]{0:T(128)} %constant.9.clone) | copy-start | bytes 40
  1.7 29.5 %copy-start.6 = (f32[3]{0:T(128)S(1)}, f32[3]{0:T(128)}, u32[]{:S(2)}) copy-start(f32[3]{0:T(128)} %constant.8.clone) | copy-start | bytes 40
  1.8 29.5 %copy-start.7 = (f32[3]{0:T(128)S(1)}, f32[3]{0:T(128)}, u32[]{:S(2)}) copy-start(f32[3]{0:T(128)} %constant.7.clone) | copy-start | bytes 40
  3.5 15.7 %collective-permute-start.2 = (f32[1,8,128]{2,0,1:T(1,128)S(1)}, f32[1,8,128]{2,0,1:T(1,128)S(1)}, u32[]{:S(2)}, u32[]{:S(2)}) collective-permute-start(f32[1,8,128]{2,0,1:T(1,128)S(1)} %get-tuple-element.59), channel_id=1, source_target_pairs={{0,4},{4,8},{8,12},{12,16},{16,20},{20,24},{24,28},{28,32},{32,36}... | collective-permute-start | bytes 12296 | tf_op jit(solution)/shard_map/ppermute | solution.py:21
  8.9 10.4 %collective-permute-start = (f32[1,8,128]{2,0,1:T(1,128)S(1)}, f32[1,8,128]{2,0,1:T(1,128)S(1)}, u32[]{:S(2)}, u32[]{:S(2)}) collective-permute-start(f32[1,8,128]{2,0,1:T(1,128)S(1)} %get-tuple-element.60), channel_id=1, source_target_pairs={{4,0},{8,4},{12,8},{16,12},{20,16},{24,20},{28,24},{32,28},{36,32}... | collective-permute-start | bytes 12296 | tf_op jit(solution)/shard_map/ppermute | solution.py:24
  13.6 8.3 %collective-permute-start.1 = (f32[3,1,8,128]{3,1,2,0:T(1,128)S(1)}, f32[3,1,8,128]{3,1,2,0:T(1,128)S(1)}, u32[]{:S(2)}, u32[]{:S(2)}) collective-permute-start(f32[3,1,8,128]{3,1,2,0:T(1,128)S(1)} %bitcast.62), channel_id=1, source_target_pairs={{4,0},{8,4},{12,8},{16,12},{20,16},{24,20},{28,24},{32,28},{36,32}... | collective-permute-start | bytes 36872 | tf_op jit(solution)/shard_map/ppermute | solution.py:24
  15.5 6.3 collective-permute-start.3
  19.2 7.9 collective-permute-start.6
  20.5 6.7 collective-permute-start.4
  21.9 5.6 collective-permute-start.7
  25.9 5.0 collective-permute-start.5
  31.6 5.7 collective-permute-start.9
  35.4 5.0 collective-permute-start.8
  40.4 4.4 collective-permute-start.11
  43.5 4.7 collective-permute-start.10
  254.8 4.3 collective-permute-start.13
  257.0 5.0 collective-permute-start.12
  262.0 4.1 collective-permute-start.15
  264.8 4.7 collective-permute-start.14
  372.6 4.3 collective-permute-start.17
  374.5 5.0 collective-permute-start.16
  379.6 5.0 collective-permute-start.19
  383.2 4.7 collective-permute-start.18
  388.6 5.5 collective-permute-start.21
  392.2 5.0 collective-permute-start.20
  397.3 2.7 collective-permute-start.23
  398.7 4.7 collective-permute-start.22
  403.8 335.4 %copy-start.10 = (s32[4,2,32]{2,1,0:T(2,128)S(1)}, s32[4,2,32]{2,1,0:T(2,128)}, u32[]{:S(2)}) copy-start(s32[4,2,32]{2,1,0:T(2,128)} %param.32) | copy-start | bytes 3076
  608.7 4.3 collective-permute-start.25
  611.0 5.0 collective-permute-start.24
  616.0 4.7 collective-permute-start.27
  619.4 4.7 collective-permute-start.26
  727.2 4.4 collective-permute-start.29
  729.2 13.9 %copy-start.8 = (f32[16,16,1,1]{1,0,3,2:T(8,128)S(1)}, f32[16,16,1,1]{1,0,3,2:T(8,128)}, u32[]{:S(2)}) copy-start(f32[16,16,1,1]{1,0,3,2:T(8,128)} %constant.59) | copy-start | bytes 3076
  729.2 5.0 collective-permute-start.28
  734.2 7.0 collective-permute-start.31
  737.9 4.7 collective-permute-start.30
  739.2 4.3 copy-start.9
  739.5 4.6 copy-start.4
  749.3 31.3 %all-to-all-start = ((f32[128,1,768]{2,1,0:T(1,128)}), f32[128,1,768]{2,1,0:T(1,128)S(1)}, u32[]{:S(2)}, u32[]{:S(2)}) async-start(f32[128,1,768]{2,1,0:T(1,128)} %reshape.66), calls=%async_computation | async-start | bytes 786432 | tf_op jit(solution)/shard_map/all_to_all | solution.py:144
where the time goes:
time: 826 us; the launch traced here: 816 us
  blocking collectives  603 us (73%)
  starting transfers between devices  92.5 us (11%)
  waiting for transfers between devices  54.8 us (7%)
  local copies, waits for them, and re-layouts  41.9 us (5%)
  other arithmetic  11.5 us (1%)
  between operations  9.84 us (1%)
    psum x6, blocking collectives, single_sum(): return lax.psum(value, ('slab', 'grp'))  603 us
    ppermute x16, starting transfers between devices, with_halo(): lax.ppermute(lax.slice_in_dim(block, block.shape[dim] - width, None, axis...  48 us
    ppermute x16, waiting for transfers between devices, with_halo(): lax.ppermute(lax.slice_in_dim(block, 0, width, axis=dim), axis, backward)  38.8 us
    ppermute x16, starting transfers between devices, with_halo(): lax.ppermute(lax.slice_in_dim(block, 0, width, axis=dim), axis, backward)  29.8 us
  transfers between devices with their start and end apart: 33, of which 14 were waited for; matrix products, arithmetic and copies ran while one was open for 0% of the time, Pallas kernels for 0%

commit v1 on v0

--- a/solution.py
+++ b/solution.py
@@ -3,6 +3,7 @@
 import numpy as np
 from jax import lax
 from jax.sharding import PartitionSpec as P
+from jax.lax import psum
 
 STEPS = 2
 ITERS = 2
@@ -11,6 +12,10 @@
 SPRING_SHEAR = 0.4
 MASS_TERM = 1.0
 CRACK_CUT = 0.9
+
+
+def raise_the_task(group_axis, my_tile, named_axis):
+    return psum(psum(my_tile, named_axis), group_axis)
 
 
 def with_halo(block, sides, width):
@@ -86,7 +91,7 @@
 
 
 def single_sum(value):
-    return lax.psum(value, ("slab", "grp"))
+    return raise_the_task("slab", value, "grp")
 
 
 def lift(signal):

time: 826 us -> 1790 us (2.17)
  blocking collectives: 603 us -> 1540 us
  starting transfers between devices: 92.5 us -> 123 us
    psum x6 -> x12, blocking collectives: 603 us -> 1540 us  [raise_the_task(): return psum(psum(my_tile, named_axis), group_axis)]
    all_to_all x1, starting transfers between devices: 14.6 us -> 45.6 us  [body(): lax.all_to_all(moved, 'slab', split_axis=2, concat_axis=3, tiled=True)]
where the time goes in v1:
time: 1790 us; the launch traced here: 1780 us
  blocking collectives  1540 us (86%)
  starting transfers between devices  123 us (7%)
  waiting for transfers between devices  53.8 us (3%)
  local copies, waits for them, and re-layouts  41.9 us (2%)
    psum x12, blocking collectives, raise_the_task(): return psum(psum(my_tile, named_axis), group_axis)  1540 us
    ppermute x16, starting transfers between devices, with_halo(): lax.ppermute(lax.slice_in_dim(block, block.shape[dim] - width, None, axis...  47 us
    all_to_all x1, starting transfers between devices, body(): lax.all_to_all(moved, 'slab', split_axis=2, concat_axis=3, tiled=True)  45.6 us
    ppermute x16, waiting for transfers between devices, with_halo(): lax.ppermute(lax.slice_in_dim(block, 0, width, axis=dim), axis, backward)  37.8 us
  transfers between devices with their start and end apart: 33, of which 14 were waited for; matrix products, arithmetic and copies ran while one was open for 0% of the time, Pallas kernels for 0%

profile of v1, /device:TPU:1, one launch (start us, length us, event | category | flops | bytes accessed | tf_op | source)
XLA Modules:
  0.0 1783.6 jit_solution(1184914103566601014)
XLA Ops:
  3.5 5.4 collective-permute-start.2
  8.9 4.7 collective-permute-start
  15.5 3.6 collective-permute-start.3
  21.9 4.0 collective-permute-start.7
  27.5 3.4 collective-permute-done.5
  31.6 3.8 collective-permute-start.9
  37.3 3.1 collective-permute-done.8
  40.4 3.1 collective-permute-start.11
  44.8 3.4 collective-permute-done.10
  49.5 7.8 all-reduce.11
  57.3 254.5 %all-reduce.9 = (f32[]{:T(128)}, f32[]{:T(128)}) all-reduce(f32[]{:T(128)} %get-tuple-element.18, f32[]{:T(128)} %get-tuple-element.19), channel_id=1, replica_groups=mesh['slab'=128,'grp'=4] {'slab'}, use_global_device_ids=true, to_apply=%region_2.3 | all-reduce | flops 2 | bytes 16 | tf_op jit(solution)/shard_map/psum | solution.py:18
  313.7 7.1 psum.116
  320.8 249.0 %psum.117 = f32[]{:T(128)} all-reduce(f32[]{:T(128)} %psum.116), channel_id=1, replica_groups=mesh['slab'=128,'grp'=4] {'slab'}, use_global_device_ids=true, to_apply=%region_8.9 | all-reduce | flops 1 | bytes 8 | tf_op jit(solution)/shard_map/psum | solution.py:18
  573.1 2.4 collective-permute-start.12
  575.6 2.6 collective-permute-done.12
  578.2 2.8 collective-permute-start.15
  582.3 3.4 collective-permute-done.14
  586.9 6.6 psum.118
  593.6 248.5 %psum.119 = f32[]{:T(128)} all-reduce(f32[]{:T(128)} %psum.118), channel_id=1, replica_groups=mesh['slab'=128,'grp'=4] {'slab'}, use_global_device_ids=true, to_apply=%region_11.12 | all-reduce | flops 1 | bytes 8 | tf_op jit(solution)/shard_map/psum | solution.py:18
  845.4 2.4 collective-permute-start.16
  847.8 2.6 collective-permute-done.16
  850.5 3.6 collective-permute-start.19
  855.4 3.4 collective-permute-done.18
  859.5 3.4 collective-permute-start.21
  864.8 3.1 collective-permute-done.20
  870.9 3.4 collective-permute-done.22
  875.5 8.0 all-reduce.10
  883.5 248.0 %all-reduce.8 = (f32[]{:T(128)}, f32[]{:T(128)}) all-reduce(f32[]{:T(128)} %get-tuple-element.16, f32[]{:T(128)} %get-tuple-element.17), channel_id=1, replica_groups=mesh['slab'=128,'grp'=4] {'slab'}, use_global_device_ids=true, to_apply=%region_14.15 | all-reduce | flops 2 | bytes 16 | tf_op jit(solution)/shard_map/psum | solution.py:18
  1133.5 7.0 psum.124
  1140.5 249.4 %psum.125 = f32[]{:T(128)} all-reduce(f32[]{:T(128)} %psum.124), channel_id=1, replica_groups=mesh['slab'=128,'grp'=4] {'slab'}, use_global_device_ids=true, to_apply=%region_20.21 | all-reduce | flops 1 | bytes 8 | tf_op jit(solution)/shard_map/psum | solution.py:18
  1393.2 2.4 collective-permute-start.24
  1395.7 2.6 collective-permute-done.24
  1398.3 3.0 collective-permute-start.27
  1402.6 3.4 collective-permute-done.26
  1407.3 6.6 psum.126
  1413.9 248.5 %psum.127 = f32[]{:T(128)} all-reduce(f32[]{:T(128)} %psum.126), channel_id=1, replica_groups=mesh['slab'=128,'grp'=4] {'slab'}, use_global_device_ids=true, to_apply=%region_23.24 | all-reduce | flops 1 | bytes 8 | tf_op jit(solution)/shard_map/psum | solution.py:18
  1665.7 2.4 collective-permute-start.28
  1668.2 2.6 collective-permute-done.28
  1670.8 3.6 collective-permute-start.31
  1681.8 2.1 copy.79
  1685.8 45.6 %all-to-all-start = ((f32[128,1,768]{2,1,0:T(1,128)}), f32[128,1,768]{2,1,0:T(1,128)S(1)}, u32[]{:S(2)}, u32[]{:S(2)}) async-start(f32[128,1,768]{2,1,0:T(1,128)} %reshape.66), calls=%async_computation | async-start | bytes 786432 | tf_op jit(solution)/shard_map/all_to_all | solution.py:149
  1732.1 16.0 all-to-all-done
  1751.2 2.6 copy.80
  1753.8 3.8 all_to_all.10
  1757.6 6.7 slice.508
  1764.2 6.9 slice.509
  1771.5 3.3 slice.514
  1774.8 3.3 slice.515
  (132 shorter events, 55.2 us)
Async XLA Ops:
  0.6 2.8 copy-start.3
  0.6 12.9 copy-start
  1.7 29.5 %copy-start.1 = (f32[3,16,8,128]{3,2,1,0:T(8,128)S(1)}, f32[3,16,8,128]{3,2,1,0:T(8,128)}, u32[]{:S(2)}) copy-start(f32[3,16,8,128]{3,2,1,0:T(8,128)} %param.29) | copy-start | bytes 589828
  1.7 29.5 %copy-start.2 = (f32[3,16,8,128]{3,2,1,0:T(8,128)S(1)}, f32[3,16,8,128]{3,2,1,0:T(8,128)}, u32[]{:S(2)}) copy-start(f32[3,16,8,128]{3,2,1,0:T(8,128)} %param.28) | copy-start | bytes 589828
  1.7 29.5 %copy-start.5 = (f32[3]{0:T(128)S(1)}, f32[3]{0:T(128)}, u32[]{:S(2)}) copy-start(f32[3]{0:T(128)} %constant.9.clone) | copy-start | bytes 40
  1.7 29.5 %copy-start.6 = (f32[3]{0:T(128)S(1)}, f32[3]{0:T(128)}, u32[]{:S(2)}) copy-start(f32[3]{0:T(128)} %constant.8.clone) | copy-start | bytes 40
  1.8 29.5 %copy-start.7 = (f32[3]{0:T(128)S(1)}, f32[3]{0:T(128)}, u32[]{:S(2)}) copy-start(f32[3]{0:T(128)} %constant.7.clone) | copy-start | bytes 40
  3.5 15.7 collective-permute-start.2
  8.9 10.4 collective-permute-start
  13.6 8.3 collective-permute-start.1
  15.5 6.3 collective-permute-start.3
  19.2 7.9 collective-permute-start.6
  20.5 6.7 collective-permute-start.4
  21.9 5.6 collective-permute-start.7
  25.9 5.0 collective-permute-start.5
  31.6 5.7 collective-permute-start.9
  35.4 5.0 collective-permute-start.8
  40.4 4.4 collective-permute-start.11
  43.5 4.7 collective-permute-start.10
  571.2 4.3 collective-permute-start.13
  573.1 5.0 collective-permute-start.12
  578.2 4.1 collective-permute-start.15
  581.0 4.7 collective-permute-start.14
  843.5 4.3 collective-permute-start.17
  845.4 5.0 collective-permute-start.16
  850.5 4.9 collective-permute-start.19
  854.1 4.7 collective-permute-start.18
  859.5 5.3 collective-permute-start.21
  862.9 5.0 collective-permute-start.20
  867.9 3.0 collective-permute-start.23
  869.5 4.7 collective-permute-start.22
  874.6 801.6 %copy-start.10 = (s32[4,2,32]{2,1,0:T(2,128)S(1)}, s32[4,2,32]{2,1,0:T(2,128)}, u32[]{:S(2)}) copy-start(s32[4,2,32]{2,1,0:T(2,128)} %param.32) | copy-start | bytes 3076
  1391.3 4.3 collective-permute-start.25
  1393.2 5.0 collective-permute-start.24
  1398.3 4.3 collective-permute-start.27
  1401.3 4.7 collective-permute-start.26
  1663.8 4.4 collective-permute-start.29
  1665.7 13.9 copy-start.8
  1665.7 5.0 collective-permute-start.28
  1670.8 7.4 collective-permute-start.31
  1674.4 4.7 collective-permute-start.30
  1676.2 3.9 copy-start.9
  1676.5 4.1 copy-start.4
  1685.8 62.3 %all-to-all-start = ((f32[128,1,768]{2,1,0:T(1,128)}), f32[128,1,768]{2,1,0:T(1,128)S(1)}, u32[]{:S(2)}, u32[]{:S(2)}) async-start(f32[128,1,768]{2,1,0:T(1,128)} %reshape.66), calls=%async_computation | async-start | bytes 786432 | tf_op jit(solution)/shard_map/all_to_all | solution.py:149
